TPU v7x, 32 devices: a whole 2x2x4 slice. The times are simulated.
32 devices in a mesh: ctx: 8 (over y, x, core), head: 4 (over z).
Axes of the slice: x: 2, y: 2, z: 4, core: 2. Of those that a mesh axis runs over, the one named last changes fastest.
Arguments:
- patches: bfloat16 [2048, 2560], P('ctx', 'head'), may hold values from -120 to 120
- merge_index: int32 [8, 2], P('ctx'), may hold values from 0 to 15, as said below
- merge_vals: bfloat16 [8, 2, 128, 128], P('ctx'), may hold values from -0.375 to 0.375
- merger_weight: bfloat16 [2560, 4096], P('head'), may hold values from -0.125 to 0.125
- proj_weight: bfloat16 [4096, 3072], P(None, 'head'), may hold values from -0.09375 to 0.09375
- frame_ids: int32 [1024], replicated, may hold values from 0 to 23, as said below
Outputs:
- attended: bfloat16 [1024, 2048], P('ctx', 'head')
Inputs may be any that keep to these rules, and one draw needn't show every extreme that they name: `merge_index`: the two entries of output block b are two different input blocks out of 2b - 1, 2b and 2b + 1, in rising order; never 2b - 1 when b is the first block of a video; always 2b - 1 when b is the first block of a slab (1 output blocks a slab) that is not the first of a video; the last output block always takes block 2b + 1. `frame_ids`: frame ids never fall along the tokens and frames never cross slabs: every slab of 128 tokens holds 3 frames, the first of 1 to 63 tokens, then frames of 64 tokens, the last one shorter.
All inputs are finite; a program needn't handle non-finite values.
Results may differ from a plain program's by a relative error of at most 0.033.
Values may be sent and summed in bfloat16 or wider, within the bound.
A program may use at most 128 MiB of HBM per device.

v0:
```python
import math

import jax
import jax.numpy as jnp
from jax import lax
from jax.sharding import PartitionSpec as P

HD = 128
QPK = 4
KV_DEV = 1
BLK = 128


def shifted(shard, axis, by):
    count = lax.axis_size(axis)
    pairs = [(i, i + by) for i in range(count) if 0 <= i + by < count]
    return lax.ppermute(shard, axis, pairs)


def body(patches, merge_index, merge_vals, merger_weight, proj_weight, frame_ids):
    slab_rows = patches.shape[0] // 2
    channels = patches.shape[1]
    blocks_dev = slab_rows // BLK
    position = lax.axis_index("ctx")
    first_devs = 5 * lax.axis_size("ctx") // 8
    first_tokens = slab_rows * first_devs
    all_tokens = frame_ids.shape[0]
    edge_block = shifted(patches[patches.shape[0] - BLK :], "ctx", 1)
    extended = jnp.concatenate([edge_block, patches], axis=0).reshape(
        2 * blocks_dev + 1, BLK, channels
    )
    local_block = merge_index - (2 * blocks_dev * position - 1)
    chosen = jnp.take(extended, local_block, axis=0)
    merged = jnp.einsum("bjrs,bjsc->brc", merge_vals, chosen, preferred_element_type=jnp.float32)
    merged = merged.astype(jnp.bfloat16).reshape(slab_rows, channels)
    partial_hidden = jnp.dot(merged, merger_weight, preferred_element_type=jnp.float32)
    hidden = lax.psum(partial_hidden.astype(jnp.bfloat16), "head").astype(jnp.float32)
    mean_square = jnp.mean(hidden * hidden, axis=-1, keepdims=True)
    normed = (hidden * lax.rsqrt(mean_square + 1e-06)).astype(jnp.bfloat16)
    projected = jnp.dot(normed, proj_weight, preferred_element_type=jnp.float32)
    projected = projected.reshape(slab_rows, KV_DEV, QPK + 2, HD)
    queries = projected[:, :, :QPK].astype(jnp.bfloat16)
    key_values = jnp.stack([projected[:, :, QPK], projected[:, :, QPK + 1]], axis=1).astype(
        jnp.bfloat16
    )
    query_index = position * slab_rows + jnp.arange(slab_rows, dtype=jnp.int32)
    query_frame = lax.dynamic_slice_in_dim(frame_ids, position * slab_rows, slab_rows)
    query_video = (position >= first_devs).astype(jnp.int32)
    score_scale = 1.0 / math.sqrt(HD)

    def attend(softmax_state, block_kv, key_index):
        key_frame = jnp.take(frame_ids, jnp.clip(key_index, 0, all_tokens - 1))
        key_video = (key_index >= first_tokens).astype(jnp.int32)
        valid = (key_index >= 0) & (key_index < all_tokens) & (key_video == query_video)
        allowed = valid[None, :] & (key_frame[None, :] <= query_frame[:, None])
        running_max, denominator, weighted = softmax_state
        scores = (
            jnp.einsum(
                "tgpd,ngd->gptn", queries, block_kv[:, 0], preferred_element_type=jnp.float32
            )
            * score_scale
        )
        screened = jnp.where(allowed, scores, -1e30)
        new_max = jnp.maximum(running_max, jnp.max(screened, axis=-1))
        factor = jnp.exp(running_max - new_max)
        weights = jnp.where(allowed, jnp.exp(screened - new_max[..., None]), 0.0)
        denominator = denominator * factor + jnp.sum(weights, axis=-1)
        product = jnp.einsum(
            "gptn,ngd->gptd",
            weights.astype(jnp.bfloat16),
            block_kv[:, 1],
            preferred_element_type=jnp.float32,
        )
        weighted = weighted * factor[..., None] + product
        return (new_max, denominator, weighted)

    def attend_rows(softmax_state, block_kv, key_index):
        total_rows = block_kv.shape[0]
        block_rows = max(slab_rows, 2048)
        for first_row in range(0, total_rows, block_rows):
            softmax_state = attend(
                softmax_state,
                block_kv[first_row : first_row + block_rows],
                key_index[first_row : first_row + block_rows],
            )
        return softmax_state

    initial = (
        jnp.full((KV_DEV, QPK, slab_rows), -1e30, jnp.float32),
        jnp.zeros((KV_DEV, QPK, slab_rows), jnp.float32),
        jnp.zeros((KV_DEV, QPK, slab_rows, HD), jnp.float32),
    )
    softmax_state = attend_rows(initial, key_values, query_index)
    gathered = key_values
    for level in range(first_devs.bit_length()):
        offset = 2**level
        arrived_slabs = min(offset, first_devs - offset)
        arrived = shifted(gathered[: arrived_slabs * slab_rows], "ctx", offset)
        slab_owner = position - offset - jnp.arange(arrived_slabs, dtype=jnp.int32)
        key_index = (
            slab_owner[:, None] * slab_rows + jnp.arange(slab_rows, dtype=jnp.int32)[None, :]
        ).reshape(-1)
        softmax_state = attend_rows(softmax_state, arrived, key_index)
        gathered = jnp.concatenate([gathered, arrived], axis=0)
    running_max, denominator, weighted = softmax_state
    attended = weighted / denominator[..., None]
    return attended.transpose(2, 0, 1, 3).reshape(slab_rows, KV_DEV * QPK * HD).astype(jnp.bfloat16)


def solution(mesh):
    return jax.shard_map(
        body,
        mesh=mesh,
        in_specs=(
            P("ctx", "head"),
            P("ctx", None),
            P("ctx", None, None, None),
            P("head", None),
            P(None, "head"),
            P(),
        ),
        out_specs=P("ctx", "head"),
        check_vma=False,
    )
```

profile of v0, /device:TPU:4, one launch (start us, length us, event | category | flops | bytes accessed | tf_op | source)
XLA Modules:
  0.0 103.5 jit_solution(11358778952088699626)
XLA Ops:
  6.5 0.0 copy-start
  6.5 0.0 copy-start.1
  6.5 0.0 all-reduce.2.cloned.1.call-start
  6.5 1.0 slice.35
  7.5 1.9 %collective-permute-start = (bf16[128,640]{1,0:T(8,128)(2,1)S(1)}, bf16[128,640]{1,0:T(8,128)(2,1)S(1)}, u32[]{:S(2)}, u32[]{:S(2)}) collective-permute-start(bf16[128,640]{1,0:T(8,128)(2,1)S(1)} %slice.35), channel_id=1, source_target_pairs={{0,4},{4,8},{8,12},{12,16},{16,20},{20,24},{24,28},{1,5},{5,9},{9,... | collective-permute-start | bytes 491528 | tf_op jit(solution)/shard_map/ppermute | solution.py:17
  9.5 1.6 %gather_fusion.2 = s32[128]{0:T(128)S(1)} fusion(s32[1024]{0:T(1024)} %param.13, s32[1024]{0:T(1024)S(1)} %pad_clamp_fusion.4), kind=kCustom, calls=%fused_computation.clone | custom fusion | bytes 1536 | tf_op jit(solution)/shard_map/jit(_take)/gather | solution.py:52
  11.2 0.1 fusion.60
  11.3 0.1 and_bitcast_fusion
  11.3 0.7 and_bitcast_fusion.1
  12.0 3.0 %collective-permute-done = bf16[128,640]{1,0:T(8,128)(2,1)S(1)} collective-permute-done((bf16[128,640]{1,0:T(8,128)(2,1)S(1)}, bf16[128,640]{1,0:T(8,128)(2,1)S(1)}, u32[]{:S(2)}, u32[]{:S(2)}) %collective-permute-start) | collective-permute-done | bytes 163872 | tf_op jit(solution)/shard_map/ppermute | solution.py:17
  15.0 1.0 pad_maximum_fusion
  16.1 0.6 gather_fusion
  16.7 0.0 copy-done
  16.7 4.9 %convolution_convert_fusion = bf16[128,4096]{1,0:T(8,128)(2,1)} fusion(bf16[640,4096]{1,0:T(8,128)(2,1)} %param.11, bf16[2,128,640]{2,1,0:T(8,128)(2,1)S(1)} %gather_fusion, pred[2]{0:T(512)(128)(4,1)S(1)} %get-tuple-element.13, bf16[1,2,128,128]{3,2,1,0:T(8,128)(2,1)S(1)} %copy-done), kind=kOutput, calls=%fused_computation.5 | convolution fusion | flops 713801728 | bytes 6684674 | tf_op jit(solution)/shard_map/dot_general | solution.py:36
  21.6 0.0 all-reduce.2.cloned.1.call-update
  21.6 0.0 copy-done.1
  21.6 0.1 dynamic_slice.3
  21.7 1.0 gather_fusion.3
  22.7 1.0 gather_fusion.4
  23.7 1.4 %gather_fusion.1 = s32[256]{0:T(256)S(1)} fusion(s32[1024]{0:T(1024)S(1)} %copy-done.1, s32[1024]{0:T(1024)S(1)} %pad_clamp_fusion.1), kind=kCustom, calls=%fused_computation.4 | custom fusion | bytes 3072 | tf_op jit(solution)/shard_map/jit(_take)/gather | solution.py:52
  25.1 0.1 and_select_fusion.3
  25.2 0.1 compare_and_fusion
  25.3 0.2 compare_and_fusion.3
  25.5 48.4 %all-reduce.2.cloned.1.call-done = bf16[128,4096]{1,0:T(8,128)(2,1)} async-done(((bf16[128,4096]{1,0:T(8,128)(2,1)}), bf16[128,4096]{1,0:T(8,128)(2,1)}) %all-reduce.2.cloned.1.call-update) | async-done | bytes 1048592 | tf_op jit(solution)/shard_map/psum | solution.py:37
  73.9 1.5 %fusion = f32[128]{0:T(128)S(1)} fusion(bf16[128,4096]{1,0:T(8,128)(2,1)} %all-reduce.2.cloned.1.call-done), kind=kLoop, calls=%fused_computation.8 | loop fusion | flops 1572736 | bytes 1049088 | tf_op jit(solution)/shard_map/reduce_sum | solution.py:38
  75.4 4.2 %convolution_convert_fusion.1 = bf16[128,768]{1,0:T(8,128)(2,1)S(1)} fusion(bf16[4096,768]{1,0:T(8,128)(2,1)} %param.12, bf16[128,4096]{1,0:T(8,128)(2,1)} %all-reduce.2.cloned.1.call-done, f32[128]{0:T(128)S(1)} %add_rsqrt_fusion), kind=kOutput, calls=%fused_computation.13 | convolution fusion | flops 806977536 | bytes 7537152 | tf_op jit(solution)/shard_map/dot_general | solution.py:40
  79.6 0.2 copy.19
  79.8 0.1 copy.44
  79.9 0.1 copy.46
  80.0 2.0 %collective-permute-start.1 = (bf16[128,2,1,128]{3,0,2,1:T(8,128)(2,1)S(1)}, bf16[128,2,1,128]{3,0,2,1:T(8,128)(2,1)S(1)}, u32[]{:S(2)}, u32[]{:S(2)}) collective-permute-start(bf16[128,2,1,128]{3,0,2,1:T(8,128)(2,1)S(1)} %pad_maximum_fusion.2), channel_id=1, source_target_pairs={{0,4},{4,8},{8,12},{12,16},{16,20},{20,24},{24,28},{1,5},{5,9},{9,... | collective-permute-start | bytes 196616 | tf_op jit(solution)/shard_map/ppermute | solution.py:17
  82.0 1.3 %collective-permute-start.3 = (bf16[128,2,1,128]{3,0,2,1:T(8,128)(2,1)S(1)}, bf16[128,2,1,128]{3,0,2,1:T(8,128)(2,1)S(1)}, u32[]{:S(2)}, u32[]{:S(2)}) collective-permute-start(bf16[128,2,1,128]{3,0,2,1:T(8,128)(2,1)S(1)} %pad_maximum_fusion.2), channel_id=1, source_target_pairs={{0,16},{4,20},{8,24},{12,28},{1,17},{5,21},{9,25},{13,29},{2,18},{... | collective-permute-start | bytes 196616 | tf_op jit(solution)/shard_map/ppermute | solution.py:17
  83.3 0.2 fusion.76
  83.5 3.0 %collective-permute-done.1 = bf16[128,2,1,128]{3,0,2,1:T(8,128)(2,1)S(1)} collective-permute-done((bf16[128,2,1,128]{3,0,2,1:T(8,128)(2,1)S(1)}, bf16[128,2,1,128]{3,0,2,1:T(8,128)(2,1)S(1)}, u32[]{:S(2)}, u32[]{:S(2)}) %collective-permute-start.1) | collective-permute-done | bytes 65568 | tf_op jit(solution)/shard_map/ppermute | solution.py:17
  86.5 2.5 %collective-permute-start.2 = (bf16[256,2,1,128]{3,0,2,1:T(8,128)(2,1)S(1)}, bf16[256,2,1,128]{3,0,2,1:T(8,128)(2,1)S(1)}, u32[]{:S(2)}, u32[]{:S(2)}) collective-permute-start(bf16[256,2,1,128]{3,0,2,1:T(8,128)(2,1)S(1)} %pad_maximum_fusion.1), channel_id=1, source_target_pairs={{0,8},{4,12},{8,16},{12,20},{16,24},{20,28},{1,9},{5,13},{9,17},{1... | collective-permute-start | bytes 393224 | tf_op jit(solution)/shard_map/ppermute | solution.py:17
  89.0 0.2 fusion.75
  89.2 0.0 collective-permute-done.3
  89.2 0.2 fusion.73
  89.4 4.9 %collective-permute-done.2 = bf16[256,2,1,128]{3,0,2,1:T(8,128)(2,1)S(1)} collective-permute-done((bf16[256,2,1,128]{3,0,2,1:T(8,128)(2,1)S(1)}, bf16[256,2,1,128]{3,0,2,1:T(8,128)(2,1)S(1)}, u32[]{:S(2)}, u32[]{:S(2)}) %collective-permute-start.2) | collective-permute-done | bytes 131104 | tf_op jit(solution)/shard_map/ppermute | solution.py:17
  94.3 0.2 fusion.74
  94.5 0.1 fusion.32
  94.6 0.1 fusion.34
  94.7 0.1 fusion.20
  94.8 0.1 fusion.36
  94.9 0.2 fusion.4
  95.1 0.2 fusion.27
  95.4 0.2 fusion.41
  95.6 0.3 fusion.14
  95.9 0.8 copy.31
  (20 shorter events, 0.2 us)
Async XLA Ops:
  6.5 10.1 %copy-start = (bf16[1,2,128,128]{3,2,1,0:T(8,128)(2,1)S(1)}, bf16[1,2,128,128]{3,2,1,0:T(8,128)(2,1)}, u32[]{:S(2)}) copy-start(bf16[1,2,128,128]{3,2,1,0:T(8,128)(2,1)} %param.10) | copy-start | bytes 196612
  6.5 15.1 %copy-start.1 = (s32[1024]{0:T(1024)S(1)}, s32[1024]{0:T(1024)}, u32[]{:S(2)}) copy-start(s32[1024]{0:T(1024)} %param.13) | copy-start | bytes 12292
  6.5 67.4 %all-reduce.2.cloned.1.call-start = ((), (), s32[]{:S(2)}) async-start(), calls=%async_computation | async-start | bytes 2097152 | tf_op jit(solution)/shard_map/psum | solution.py:37
  7.5 7.5 %collective-permute-start = (bf16[128,640]{1,0:T(8,128)(2,1)S(1)}, bf16[128,640]{1,0:T(8,128)(2,1)S(1)}, u32[]{:S(2)}, u32[]{:S(2)}) collective-permute-start(bf16[128,640]{1,0:T(8,128)(2,1)S(1)} %slice.35), channel_id=1, source_target_pairs={{0,4},{4,8},{8,12},{12,16},{16,20},{20,24},{24,28},{1,5},{5,9},{9,... | collective-permute-start | bytes 491528 | tf_op jit(solution)/shard_map/ppermute | solution.py:17
  80.0 6.5 %collective-permute-start.1 = (bf16[128,2,1,128]{3,0,2,1:T(8,128)(2,1)S(1)}, bf16[128,2,1,128]{3,0,2,1:T(8,128)(2,1)S(1)}, u32[]{:S(2)}, u32[]{:S(2)}) collective-permute-start(bf16[128,2,1,128]{3,0,2,1:T(8,128)(2,1)S(1)} %pad_maximum_fusion.2), channel_id=1, source_target_pairs={{0,4},{4,8},{8,12},{12,16},{16,20},{20,24},{24,28},{1,5},{5,9},{9,... | collective-permute-start | bytes 196616 | tf_op jit(solution)/shard_map/ppermute | solution.py:17
  82.0 7.2 %collective-permute-start.3 = (bf16[128,2,1,128]{3,0,2,1:T(8,128)(2,1)S(1)}, bf16[128,2,1,128]{3,0,2,1:T(8,128)(2,1)S(1)}, u32[]{:S(2)}, u32[]{:S(2)}) collective-permute-start(bf16[128,2,1,128]{3,0,2,1:T(8,128)(2,1)S(1)} %pad_maximum_fusion.2), channel_id=1, source_target_pairs={{0,16},{4,20},{8,24},{12,28},{1,17},{5,21},{9,25},{13,29},{2,18},{... | collective-permute-start | bytes 196616 | tf_op jit(solution)/shard_map/ppermute | solution.py:17
  86.5 7.8 %collective-permute-start.2 = (bf16[256,2,1,128]{3,0,2,1:T(8,128)(2,1)S(1)}, bf16[256,2,1,128]{3,0,2,1:T(8,128)(2,1)S(1)}, u32[]{:S(2)}, u32[]{:S(2)}) collective-permute-start(bf16[256,2,1,128]{3,0,2,1:T(8,128)(2,1)S(1)} %pad_maximum_fusion.1), channel_id=1, source_target_pairs={{0,8},{4,12},{8,16},{12,20},{16,24},{20,28},{1,9},{5,13},{9,17},{1... | collective-permute-start | bytes 393224 | tf_op jit(solution)/shard_map/ppermute | solution.py:17
Sparse Core Ops, SparseCore 0:
  21.7 52.1 all-reduce.1
where the time goes:
time: 104 us; the launch traced here: 103 us
  waiting for transfers between devices  59.3 us (57%)
  between operations  13.7 us (13%)
  matrix products  10.8 us (10%)
  local copies, waits for them, and re-layouts  7.75 us (7%)
  starting transfers between devices  7.64 us (7%)
  other arithmetic  4.21 us (4%)
    psum x1, waiting for transfers between devices, body(): lax.psum(partial_hidden.astype(jnp.bfloat16), 'head').astype(jnp.float32)  48.4 us
    ppermute x4, waiting for transfers between devices, shifted(): return lax.ppermute(shard, axis, pairs)  10.9 us
    ppermute x4, starting transfers between devices, shifted(): return lax.ppermute(shard, axis, pairs)  7.64 us
    gather x4, local copies, waits for them, and re-layouts, attend(): key_frame = jnp.take(frame_ids, jnp.clip(key_index, 0, all_tokens - 1))  4.92 us
    dot_general x1, matrix products, body(): jnp.dot(merged, merger_weight, preferred_element_type=jnp.float32)  4.91 us
    dot_general x1, matrix products, body(): projected = jnp.dot(normed, proj_weight, preferred_element_type=jnp.float32)  4.16 us
  transfers between devices with their start and end apart: 5, of which 4 were waited for; matrix products, arithmetic and copies ran while one was open for 7% of the time, Pallas kernels for 0%

commit v1 on v0

v1 whole, which is shorter than its diff:
```python
import functools
import math

import jax
import jax.numpy as jnp
from jax import lax
from jax.experimental import pallas as pl
from jax.experimental.pallas import tpu as pltpu
from jax.sharding import PartitionSpec as P

HD = 128
QPK = 4
BLK = 128
CHUNK = 256
LAG = 2
MESH = pl.DeviceIdType.MESH


def remote(src, dst, send_sem, recv_sem, target):
    return pltpu.make_async_remote_copy(
        src_ref=src,
        dst_ref=dst,
        send_sem=send_sem,
        recv_sem=recv_sem,
        device_id=target,
        device_id_type=MESH,
    )


def kernel(
    ctx_size,
    index_ref,
    frames_ref,
    vals_hbm,
    patches,
    merger,
    proj,
    out_ref,
    vals,
    own,
    edge,
    merger_v,
    proj_v,
    merged,
    part,
    inward,
    outward,
    from_outer,
    from_inner,
    projected,
    squares,
    queries,
    kv_own,
    kv_in,
    vals_sem,
    own_sem,
    merger_sem,
    proj_sem,
    edge_send,
    edge_recv,
    in_send,
    out_send,
    outer_recv,
    inner_recv,
    kv_send,
    kv_recv,
):
    chunks = merger_v.shape[0]
    hid = chunks * CHUNK
    rows = merged.shape[0]
    position = lax.axis_index("ctx")
    plane = lax.axis_index("head")
    first_devs = 5 * ctx_size // 8
    in_first = position < first_devs
    video_start = jnp.where(in_first, 0, first_devs)
    video_size = jnp.where(in_first, first_devs, ctx_size - first_devs)
    earlier = position - video_start
    later = video_size - 1 - earlier
    is_outer = (plane == 0) | (plane == 3)
    inner = jnp.where(plane < 2, plane + 1, plane - 1)
    outer = jnp.where(plane == 1, 0, 3)

    own_copy = pltpu.make_async_copy(patches, own, own_sem)
    own_copy.start()
    vals_copy = pltpu.make_async_copy(vals_hbm, vals, vals_sem)
    vals_copy.start()

    def merger_copy(c):
        columns = pl.ds(pl.multiple_of(c * CHUNK, CHUNK), CHUNK)
        return pltpu.make_async_copy(merger.at[:, columns], merger_v.at[c], merger_sem.at[c])

    def proj_copy(c):
        depth = pl.ds(pl.multiple_of(c * CHUNK, CHUNK), CHUNK)
        return pltpu.make_async_copy(proj.at[depth, :], proj_v.at[c], proj_sem.at[c])

    barrier = pltpu.get_barrier_semaphore()

    @pl.loop(0, video_size)
    def _(i):
        @pl.when(video_start + i != position)
        def _():
            pl.semaphore_signal(
                barrier, inc=1, device_id={"ctx": video_start + i}, device_id_type=MESH
            )

    pl.semaphore_signal(barrier, inc=1, device_id={"head": inner}, device_id_type=MESH)

    @pl.when(jnp.logical_not(is_outer))
    def _():
        pl.semaphore_signal(barrier, inc=1, device_id={"head": outer}, device_id_type=MESH)

    @pl.loop(0, chunks)
    def _(c):
        merger_copy(c).start()

    pl.semaphore_wait(barrier, video_size - 1 + jnp.where(is_outer, 1, 2))

    def edge_copy():
        return remote(
            patches.at[pl.ds(BLK, BLK), :], edge, edge_send, edge_recv, {"ctx": position + 1}
        )

    @pl.when(later > 0)
    def _():
        edge_copy().start()

    @pl.loop(0, chunks)
    def _(c):
        proj_copy(c).start()

    projected[...] = jnp.zeros_like(projected)
    squares[...] = jnp.zeros_like(squares)

    own_copy.wait()
    vals_copy.wait()
    lower_first = (index_ref[0, 0] == 2 * position).astype(jnp.float32)
    upper_second = (index_ref[0, 1] - 2 * position).astype(jnp.float32)
    lower_vals = vals[0].astype(jnp.float32)
    upper_vals = vals[1].astype(jnp.float32)
    own_vals = jnp.concatenate(
        [lower_vals * lower_first + upper_vals * (1.0 - upper_second), upper_vals * upper_second],
        axis=1,
    )
    own_sum = jnp.dot(own_vals.astype(jnp.bfloat16), own[...], preferred_element_type=jnp.float32)

    @pl.when(earlier == 0)
    def _():
        merged[...] = own_sum.astype(jnp.bfloat16)

    @pl.when(earlier > 0)
    def _():
        edge_copy().wait_recv()
        edge_sum = jnp.dot(vals[0], edge[...], preferred_element_type=jnp.float32)
        merged[...] = (edge_sum + own_sum).astype(jnp.bfloat16)

    def partial_hidden(c):
        merger_copy(c).wait()
        return jnp.dot(merged[...], merger_v[c], preferred_element_type=jnp.float32)

    def project(c, hidden):
        hidden = hidden.astype(jnp.bfloat16)
        wide = hidden.astype(jnp.float32)
        wide = wide * wide
        total = wide[:, :128]
        for at in range(128, CHUNK, 128):
            total = total + wide[:, at : at + 128]
        squares[...] += total
        proj_copy(c).wait()
        projected[...] += jnp.dot(hidden, proj_v[c], preferred_element_type=jnp.float32)

    def to_mid_from_outer(c):
        return remote(
            inward.at[c], from_outer.at[c], in_send.at[c], outer_recv.at[c], {"head": inner}
        )

    def to_mid_from_mid(c):
        return remote(
            inward.at[c], from_inner.at[c], in_send.at[c], inner_recv.at[c], {"head": inner}
        )

    def to_outer(c):
        return remote(
            outward.at[c], from_inner.at[c], out_send.at[c], inner_recv.at[c], {"head": outer}
        )

    @pl.when(is_outer)
    def _():
        @pl.loop(0, chunks)
        def _(c):
            hidden = partial_hidden(c)
            part[c] = hidden
            inward[c] = hidden.astype(jnp.bfloat16)
            to_mid_from_outer(c).start()

        @pl.loop(0, chunks)
        def _(c):
            to_mid_from_mid(c).wait_recv()
            project(c, part[c] + from_inner[c].astype(jnp.float32))

        @pl.loop(0, chunks)
        def _(c):
            to_mid_from_outer(c).wait_send()

    @pl.when(jnp.logical_not(is_outer))
    def _():
        def forward_in(c):
            hidden = partial_hidden(c)
            part[c] = hidden
            to_mid_from_outer(c).wait_recv()
            inward[c] = (hidden + from_outer[c].astype(jnp.float32)).astype(jnp.bfloat16)
            to_mid_from_mid(c).start()

        def forward_out(c):
            to_mid_from_mid(c).wait_recv()
            hidden = part[c] + from_inner[c].astype(jnp.float32)
            outward[c] = hidden.astype(jnp.bfloat16)
            to_outer(c).start()
            project(c, hidden + from_outer[c].astype(jnp.float32))

        @pl.loop(0, LAG)
        def _(c):
            forward_in(c)

        @pl.loop(LAG, chunks)
        def _(c):
            forward_in(c)
            forward_out(c - LAG)

        @pl.loop(chunks - LAG, chunks)
        def _(c):
            forward_out(c)

        @pl.loop(0, chunks)
        def _(c):
            to_mid_from_mid(c).wait_send()
            to_outer(c).wait_send()

    mean_square = jnp.sum(squares[...], axis=1, keepdims=True) * (1.0 / hid)
    gain = lax.rsqrt(mean_square + 1e-06)
    kv_own[...] = (projected[:, QPK * HD :] * gain).astype(jnp.bfloat16)

    def kv_copy(d):
        return remote(
            kv_own, kv_in.at[d], kv_send.at[d], kv_recv.at[d], {"ctx": position + 1 + d}
        )

    @pl.loop(0, later)
    def _(d):
        kv_copy(d).start()

    for p in range(QPK):
        queries[p * rows : (p + 1) * rows, :] = (
            projected[:, p * HD : (p + 1) * HD] * gain
        ).astype(jnp.bfloat16)

    score_scale = 1.0 / math.sqrt(HD)

    def score(keys):
        return (
            lax.dot_general(
                queries[...], keys, (((1,), (1,)), ((), ())), preferred_element_type=jnp.float32
            )
            * score_scale
        )

    key_frame = jnp.broadcast_to(frames_ref[pl.ds(position, 1), :], (rows, rows)).astype(
        jnp.float32
    )
    query_frame = jnp.transpose(key_frame)
    allowed = key_frame <= query_frame
    allowed = jnp.concatenate([allowed.astype(jnp.float32)] * QPK, axis=0) > 0.5
    scores = jnp.where(allowed, score(kv_own[:, :HD]), -1e30)
    top = jnp.max(scores, axis=1, keepdims=True)
    weights = jnp.where(allowed, jnp.exp(scores - top), 0.0)
    total = jnp.sum(weights, axis=1, keepdims=True)
    mixed = jnp.dot(
        weights.astype(jnp.bfloat16), kv_own[:, HD:], preferred_element_type=jnp.float32
    )

    def attend(d, state):
        top, total, mixed = state
        kv_copy(d).wait_recv()
        scores = score(kv_in[d, :, :HD])
        new_top = jnp.maximum(top, jnp.max(scores, axis=1, keepdims=True))
        factor = jnp.exp(top - new_top)
        weights = jnp.exp(scores - new_top)
        total = total * factor + jnp.sum(weights, axis=1, keepdims=True)
        mixed = mixed * factor + jnp.dot(
            weights.astype(jnp.bfloat16), kv_in[d, :, HD:], preferred_element_type=jnp.float32
        )
        return new_top, total, mixed

    top, total, mixed = lax.fori_loop(0, earlier, attend, (top, total, mixed))
    attended = (mixed / total).astype(jnp.bfloat16)
    for p in range(QPK):
        out_ref[:, p * HD : (p + 1) * HD] = attended[p * rows : (p + 1) * rows, :]

    @pl.loop(0, later)
    def _(d):
        kv_copy(d).wait_send()

    @pl.when(later > 0)
    def _():
        edge_copy().wait_send()


def body(ctx_size, patches, merge_index, merge_vals, merger_weight, proj_weight, frame_ids):
    rows = patches.shape[0] // 2
    channels = patches.shape[1]
    hid = merger_weight.shape[1]
    width = proj_weight.shape[1]
    chunks = hid // CHUNK
    most = 5 * ctx_size // 8 - 1
    bf16, f32 = jnp.bfloat16, jnp.float32
    sem = pltpu.SemaphoreType.DMA
    any_space = pl.BlockSpec(memory_space=pl.ANY)
    return pl.pallas_call(
        functools.partial(kernel, ctx_size),
        out_shape=jax.ShapeDtypeStruct((rows, QPK * HD), bf16),
        in_specs=[
            pl.BlockSpec(memory_space=pltpu.SMEM),
            pl.BlockSpec(memory_space=pltpu.VMEM),
            any_space,
            any_space,
            any_space,
            any_space,
        ],
        out_specs=pl.BlockSpec(memory_space=pltpu.VMEM),
        scratch_shapes=[
            pltpu.VMEM((2, BLK, BLK), bf16),
            pltpu.VMEM((2 * rows, channels), bf16),
            pltpu.VMEM((BLK, channels), bf16),
            pltpu.VMEM((chunks, channels, CHUNK), bf16),
            pltpu.VMEM((chunks, CHUNK, width), bf16),
            pltpu.VMEM((rows, channels), bf16),
            pltpu.VMEM((chunks, rows, CHUNK), f32),
            pltpu.VMEM((chunks, rows, CHUNK), bf16),
            pltpu.VMEM((chunks, rows, CHUNK), bf16),
            pltpu.VMEM((chunks, rows, CHUNK), bf16),
            pltpu.VMEM((chunks, rows, CHUNK), bf16),
            pltpu.VMEM((rows, width), f32),
            pltpu.VMEM((rows, 128), f32),
            pltpu.VMEM((QPK * rows, HD), bf16),
            pltpu.VMEM((rows, 2 * HD), bf16),
            pltpu.VMEM((most, rows, 2 * HD), bf16),
            sem,
            sem,
            sem((chunks,)),
            sem((chunks,)),
            sem,
            sem,
            sem((chunks,)),
            sem((chunks,)),
            sem((chunks,)),
            sem((chunks,)),
            sem((most,)),
            sem((most,)),
        ],
        compiler_params=pltpu.CompilerParams(
            collective_id=0, has_side_effects=True, vmem_limit_bytes=62 * 2**20
        ),
        cost_estimate=pl.CostEstimate(
            flops=4 * 10**9, bytes_accessed=12 * 10**6, transcendentals=4 * 10**5
        ),
        name="slab",
    )(
        merge_index,
        frame_ids.reshape(ctx_size, rows),
        merge_vals[0],
        patches,
        merger_weight,
        proj_weight,
    )


def solution(mesh):
    return jax.shard_map(
        functools.partial(body, mesh.shape["ctx"]),
        mesh=mesh,
        in_specs=(
            P("ctx", "head"),
            P("ctx", None),
            P("ctx", None, None, None),
            P("head", None),
            P(None, "head"),
            P(),
        ),
        out_specs=P("ctx", "head"),
        check_vma=False,
    )
```

time: 104 us -> 48.1 us (0.46)
  waiting for transfers between devices: 59.3 us -> 0 us
  Pallas kernels: 0 us -> 46.4 us
  between operations: 13.7 us -> 0.01 us
  matrix products: 10.8 us -> 0 us
  starting transfers between devices: 7.64 us -> 0 us
  local copies, waits for them, and re-layouts: 7.75 us -> 1.57 us
  other arithmetic: 4.21 us -> 0 us
    psum x1 -> x0, waiting for transfers between devices: 48.4 us -> none  [body(): lax.psum(partial_hidden.astype(jnp.bfloat16), 'head').astype(jnp.float32)]
    pallas_call x0 -> x1, Pallas kernels: none -> 46.4 us  [body(): pl.pallas_call(functools.partial(kernel, ctx_size), out_shape=jax.ShapeDt...]
    ppermute x4 -> x0, waiting for transfers between devices: 10.9 us -> none  [shifted(): return lax.ppermute(shard, axis, pairs)]
    dot_general x10 -> x0, matrix products: 10.8 us -> none  [the longest x1 4.91 us: body(): jnp.dot(merged, merger_weight, preferred_element_type=jnp.float32)]
    ppermute x4 -> x0, starting transfers between devices: 7.64 us -> none  [shifted(): return lax.ppermute(shard, axis, pairs)]
    gather x5 -> x0, local copies, waits for them, and re-layouts: 5.53 us -> none  [the longest x4 4.92 us: attend(): key_frame = jnp.take(frame_ids, jnp.clip(key_index, 0, all_tokens - 1))]
    reduce_sum x5 -> x0, other arithmetic: 1.84 us -> none  [the longest x1 1.52 us: body(): mean_square = jnp.mean(hidden * hidden, axis=-1, keepdims=True)]
    unnamed x6 -> x1, local copies, waits for them, and re-layouts: 0.24 us -> 1.57 us
  transfers between devices with their start and end apart: 5 -> 0, of which waited for: 4 -> 0; matrix products, arithmetic and copies ran while one was open for 7% -> 0% of each run, Pallas kernels for 0% -> 0%
where the time goes in v1:
time: 48.1 us; the launch traced here: 47.9 us
  Pallas kernels  46.4 us (96%)
  local copies, waits for them, and re-layouts  1.57 us (3%)
    pallas_call x1, Pallas kernels, body(): pl.pallas_call(functools.partial(kernel, ctx_size), out_shape=jax.ShapeDt...  46.4 us
    unnamed x1, local copies, waits for them, and re-layouts  1.57 us

profile of v1, /device:TPU:4, one launch (start us, length us, event | category | flops | bytes accessed | tf_op | source)
XLA Modules:
  0.0 47.9 jit_solution(8836152597628613207)
XLA Ops:
  0.0 46.4 %slab.1 = bf16[128,512]{1,0:T(8,128)(2,1)} custom-call(s32[1,2]{1,0:T(1,128)} %index_ref.1, s32[8,128]{1,0:T(8,128)} %bitcast.3, bf16[2,128,128]{2,1,0:T(8,128)(2,1)} %bitcast.2, bf16[256,640]{1,0:T(8,128)(2,1)} %patches.1, bf16[640,4096]{1,0:T(8,128)(2,1)} %merger.1, bf16[4096,768]{1,0:T(8,128)(2,1)} %proj.1), custom_call_target="tpu_custom_call" | custom-call | flops 4000000000 | bytes 12000000 | tf_op jit(solution)/shard_map/slab/pallas_call | solution.py:317
  46.4 1.6 %copy.8 = bf16[128,512]{1,0:T(8,128)(2,1)} copy(bf16[128,512]{1,0:T(8,128)(2,1)} %slab.1) | data formatting | bytes 262144

commit v2 on v1

--- a/solution.py
+++ b/solution.py
@@ -11,7 +11,8 @@
 HD = 128
 QPK = 4
 BLK = 128
-CHUNK = 256
+CHUNK = 512
+HALVES = 2
 LAG = 2
 MESH = pl.DeviceIdType.MESH
 
@@ -65,9 +66,11 @@
     kv_send,
     kv_recv,
 ):
-    chunks = merger_v.shape[0]
-    hid = chunks * CHUNK
+    pieces = merger_v.shape[0]
+    chunks = HALVES * pieces
+    hid = pieces * CHUNK
     rows = merged.shape[0]
+    part_rows = rows // HALVES
     position = lax.axis_index("ctx")
     plane = lax.axis_index("head")
     first_devs = 5 * ctx_size // 8
@@ -109,9 +112,9 @@
     def _():
         pl.semaphore_signal(barrier, inc=1, device_id={"head": outer}, device_id_type=MESH)
 
-    @pl.loop(0, chunks)
-    def _(c):
-        merger_copy(c).start()
+    @pl.loop(0, pieces)
+    def _(j):
+        merger_copy(j).start()
 
     pl.semaphore_wait(barrier, video_size - 1 + jnp.where(is_outer, 1, 2))
 
@@ -124,9 +127,9 @@
     def _():
         edge_copy().start()
 
-    @pl.loop(0, chunks)
-    def _(c):
-        proj_copy(c).start()
+    @pl.loop(0, pieces)
+    def _(j):
+        proj_copy(j).start()
 
     projected[...] = jnp.zeros_like(projected)
     squares[...] = jnp.zeros_like(squares)
@@ -153,20 +156,61 @@
         edge_sum = jnp.dot(vals[0], edge[...], preferred_element_type=jnp.float32)
         merged[...] = (edge_sum + own_sum).astype(jnp.bfloat16)
 
+    def part_span(h):
+        return pl.ds(pl.multiple_of(h * part_rows, part_rows), part_rows)
+
     def partial_hidden(c):
-        merger_copy(c).wait()
-        return jnp.dot(merged[...], merger_v[c], preferred_element_type=jnp.float32)
+        h, j = c // pieces, c % pieces
+
+        @pl.when(h == 0)
+        def _():
+            merger_copy(j).wait()
+
+        return jnp.dot(
+            merged[part_span(h), :], merger_v[j], preferred_element_type=jnp.float32
+        )
+
+    def kv_copy(d, h):
+        return remote(
+            kv_own.at[part_span(h), :],
+            kv_in.at[d, part_span(h), :],
+            kv_send.at[HALVES * d + h],
+            kv_recv.at[HALVES * d + h],
+            {"ctx": position + 1 + d},
+        )
+
+    def finish(h):
+        mean_square = jnp.sum(squares[h], axis=1, keepdims=True) * (1.0 / hid)
+        gain = lax.rsqrt(mean_square + 1e-06)
+        kv_own[part_span(h), :] = (projected[h, :, QPK * HD :] * gain).astype(jnp.bfloat16)
+
+        @pl.loop(0, later)
+        def _(d):
+            kv_copy(d, h).start()
+
+        for p in range(QPK):
+            at = pl.ds(pl.multiple_of(p * rows + h * part_rows, part_rows), part_rows)
+            queries[at, :] = (projected[h, :, p * HD : (p + 1) * HD] * gain).astype(jnp.bfloat16)
 
     def project(c, hidden):
+        h, j = c // pieces, c % pieces
         hidden = hidden.astype(jnp.bfloat16)
         wide = hidden.astype(jnp.float32)
         wide = wide * wide
         total = wide[:, :128]
         for at in range(128, CHUNK, 128):
             total = total + wide[:, at : at + 128]
-        squares[...] += total
-        proj_copy(c).wait()
-        projected[...] += jnp.dot(hidden, proj_v[c], preferred_element_type=jnp.float32)
+        squares[h] += total
+
+        @pl.when(h == 0)
+        def _():
+            proj_copy(j).wait()
+
+        projected[h] += jnp.dot(hidden, proj_v[j], preferred_element_type=jnp.float32)
+
+        @pl.when(j == pieces - 1)
+        def _():
+            finish(h)
 
     def to_mid_from_outer(c):
         return remote(
@@ -235,69 +279,60 @@
             to_mid_from_mid(c).wait_send()
             to_outer(c).wait_send()
 
-    mean_square = jnp.sum(squares[...], axis=1, keepdims=True) * (1.0 / hid)
-    gain = lax.rsqrt(mean_square + 1e-06)
-    kv_own[...] = (projected[:, QPK * HD :] * gain).astype(jnp.bfloat16)
-
-    def kv_copy(d):
-        return remote(
-            kv_own, kv_in.at[d], kv_send.at[d], kv_recv.at[d], {"ctx": position + 1 + d}
-        )
-
-    @pl.loop(0, later)
-    def _(d):
-        kv_copy(d).start()
-
-    for p in range(QPK):
-        queries[p * rows : (p + 1) * rows, :] = (
-            projected[:, p * HD : (p + 1) * HD] * gain
-        ).astype(jnp.bfloat16)
-
     score_scale = 1.0 / math.sqrt(HD)
 
     def score(keys):
         return (
             lax.dot_general(
-                queries[...], keys, (((1,), (1,)), ((), ())), preferred_element_type=jnp.float32
+                keys, queries[...], (((1,), (1,)), ((), ())), preferred_element_type=jnp.float32
             )
             * score_scale
         )
 
-    key_frame = jnp.broadcast_to(frames_ref[pl.ds(position, 1), :], (rows, rows)).astype(
+    def mix(values, weights):
+        return lax.dot_general(
+            values,
+            weights.astype(jnp.bfloat16),
+            (((0,), (0,)), ((), ())),
+            preferred_element_type=jnp.float32,
+        )
+
+    query_frame = jnp.broadcast_to(frames_ref[pl.ds(position, 1), :], (rows, rows)).astype(
         jnp.float32
     )
-    query_frame = jnp.transpose(key_frame)
-    allowed = key_frame <= query_frame
-    allowed = jnp.concatenate([allowed.astype(jnp.float32)] * QPK, axis=0) > 0.5
+    key_frame = jnp.transpose(query_frame)
+    allowed = jnp.concatenate([key_frame] * QPK, axis=1) <= jnp.concatenate(
+        [query_frame] * QPK, axis=1
+    )
     scores = jnp.where(allowed, score(kv_own[:, :HD]), -1e30)
-    top = jnp.max(scores, axis=1, keepdims=True)
+    top = jnp.max(scores, axis=0, keepdims=True)
     weights = jnp.where(allowed, jnp.exp(scores - top), 0.0)
-    total = jnp.sum(weights, axis=1, keepdims=True)
-    mixed = jnp.dot(
-        weights.astype(jnp.bfloat16), kv_own[:, HD:], preferred_element_type=jnp.float32
-    )
+    total = jnp.sum(weights, axis=0, keepdims=True)
+    mixed = mix(kv_own[:, HD:], weights)
 
     def attend(d, state):
         top, total, mixed = state
-        kv_copy(d).wait_recv()
+        for h in range(HALVES):
+            kv_copy(d, h).wait_recv()
         scores = score(kv_in[d, :, :HD])
-        new_top = jnp.maximum(top, jnp.max(scores, axis=1, keepdims=True))
+        new_top = jnp.maximum(top, jnp.max(scores, axis=0, keepdims=True))
         factor = jnp.exp(top - new_top)
         weights = jnp.exp(scores - new_top)
-        total = total * factor + jnp.sum(weights, axis=1, keepdims=True)
-        mixed = mixed * factor + jnp.dot(
-            weights.astype(jnp.bfloat16), kv_in[d, :, HD:], preferred_element_type=jnp.float32
-        )
+        total = total * factor + jnp.sum(weights, axis=0, keepdims=True)
+        mixed = mixed * factor + mix(kv_in[d, :, HD:], weights)
         return new_top, total, mixed
 
     top, total, mixed = lax.fori_loop(0, earlier, attend, (top, total, mixed))
-    attended = (mixed / total).astype(jnp.bfloat16)
+    attended = mixed / total
     for p in range(QPK):
-        out_ref[:, p * HD : (p + 1) * HD] = attended[p * rows : (p + 1) * rows, :]
+        out_ref[:, p * HD : (p + 1) * HD] = jnp.transpose(
+            attended[:, p * rows : (p + 1) * rows]
+        ).astype(jnp.bfloat16)
 
     @pl.loop(0, later)
     def _(d):
-        kv_copy(d).wait_send()
+        for h in range(HALVES):
+            kv_copy(d, h).wait_send()
 
     @pl.when(later > 0)
     def _():
@@ -309,7 +344,9 @@
     channels = patches.shape[1]
     hid = merger_weight.shape[1]
     width = proj_weight.shape[1]
-    chunks = hid // CHUNK
+    pieces = hid // CHUNK
+    chunks = HALVES * pieces
+    part_rows = rows // HALVES
     most = 5 * ctx_size // 8 - 1
     bf16, f32 = jnp.bfloat16, jnp.float32
     sem = pltpu.SemaphoreType.DMA
@@ -330,31 +367,31 @@
             pltpu.VMEM((2, BLK, BLK), bf16),
             pltpu.VMEM((2 * rows, channels), bf16),
             pltpu.VMEM((BLK, channels), bf16),
-            pltpu.VMEM((chunks, channels, CHUNK), bf16),
-            pltpu.VMEM((chunks, CHUNK, width), bf16),
+            pltpu.VMEM((pieces, channels, CHUNK), bf16),
+            pltpu.VMEM((pieces, CHUNK, width), bf16),
             pltpu.VMEM((rows, channels), bf16),
-            pltpu.VMEM((chunks, rows, CHUNK), f32),
-            pltpu.VMEM((chunks, rows, CHUNK), bf16),
-            pltpu.VMEM((chunks, rows, CHUNK), bf16),
-            pltpu.VMEM((chunks, rows, CHUNK), bf16),
-            pltpu.VMEM((chunks, rows, CHUNK), bf16),
-            pltpu.VMEM((rows, width), f32),
-            pltpu.VMEM((rows, 128), f32),
+            pltpu.VMEM((chunks, part_rows, CHUNK), f32),
+            pltpu.VMEM((chunks, part_rows, CHUNK), bf16),
+            pltpu.VMEM((chunks, part_rows, CHUNK), bf16),
+            pltpu.VMEM((chunks, part_rows, CHUNK), bf16),
+            pltpu.VMEM((chunks, part_rows, CHUNK), bf16),
+            pltpu.VMEM((HALVES, part_rows, width), f32),
+            pltpu.VMEM((HALVES, part_rows, 128), f32),
             pltpu.VMEM((QPK * rows, HD), bf16),
             pltpu.VMEM((rows, 2 * HD), bf16),
             pltpu.VMEM((most, rows, 2 * HD), bf16),
             sem,
             sem,
-            sem((chunks,)),
-            sem((chunks,)),
+            sem((pieces,)),
+            sem((pieces,)),
             sem,
             sem,
             sem((chunks,)),
             sem((chunks,)),
             sem((chunks,)),
             sem((chunks,)),
-            sem((most,)),
-            sem((most,)),
+            sem((HALVES * most,)),
+            sem((HALVES * most,)),
         ],
         compiler_params=pltpu.CompilerParams(
             collective_id=0, has_side_effects=True, vmem_limit_bytes=62 * 2**20

time: 48.1 us -> 47.7 us (level)
  Pallas kernels: 46.4 us -> 45.9 us
where the time goes in v2:
time: 47.7 us; the launch traced here: 47.5 us
  Pallas kernels  45.9 us (96%)
  local copies, waits for them, and re-layouts  1.57 us (3%)
    pallas_call x1, Pallas kernels, body(): pl.pallas_call(functools.partial(kernel, ctx_size), out_shape=jax.ShapeDt...  45.9 us
    unnamed x1, local copies, waits for them, and re-layouts  1.57 us

profile of v2, /device:TPU:4, one launch (start us, length us, event | category | flops | bytes accessed | tf_op | source)
XLA Modules:
  0.0 47.5 jit_solution(564359501937994022)
XLA Ops:
  0.0 45.9 %slab.1 = bf16[128,512]{1,0:T(8,128)(2,1)} custom-call(s32[1,2]{1,0:T(1,128)} %index_ref.1, s32[8,128]{1,0:T(8,128)} %bitcast.3, bf16[2,128,128]{2,1,0:T(8,128)(2,1)} %bitcast.2, bf16[256,640]{1,0:T(8,128)(2,1)} %patches.1, bf16[640,4096]{1,0:T(8,128)(2,1)} %merger.1, bf16[4096,768]{1,0:T(8,128)(2,1)} %proj.1), custom_call_target="tpu_custom_call" | custom-call | flops 4000000000 | bytes 12000000 | tf_op jit(solution)/shard_map/slab/pallas_call | solution.py:354
  45.9 1.6 %copy.8 = bf16[128,512]{1,0:T(8,128)(2,1)} copy(bf16[128,512]{1,0:T(8,128)(2,1)} %slab.1) | data formatting | bytes 262144

commit v3 on v2

--- a/solution.py
+++ b/solution.py
@@ -13,7 +13,8 @@
 BLK = 128
 CHUNK = 512
 HALVES = 2
-LAG = 2
+LAG = 3
+LEAD = 4
 MESH = pl.DeviceIdType.MESH
 
 
@@ -112,20 +113,20 @@
     def _():
         pl.semaphore_signal(barrier, inc=1, device_id={"head": outer}, device_id_type=MESH)
 
+    pl.semaphore_wait(barrier, video_size - 1 + jnp.where(is_outer, 1, 2))
+
+    def edge_copy():
+        return remote(
+            patches.at[pl.ds(BLK, BLK), :], edge, edge_send, edge_recv, {"ctx": position + 1}
+        )
+
+    @pl.when(later > 0)
+    def _():
+        edge_copy().start()
+
     @pl.loop(0, pieces)
     def _(j):
         merger_copy(j).start()
-
-    pl.semaphore_wait(barrier, video_size - 1 + jnp.where(is_outer, 1, 2))
-
-    def edge_copy():
-        return remote(
-            patches.at[pl.ds(BLK, BLK), :], edge, edge_send, edge_recv, {"ctx": position + 1}
-        )
-
-    @pl.when(later > 0)
-    def _():
-        edge_copy().start()
 
     @pl.loop(0, pieces)
     def _(j):
@@ -247,32 +248,41 @@
 
     @pl.when(jnp.logical_not(is_outer))
     def _():
-        def forward_in(c):
-            hidden = partial_hidden(c)
-            part[c] = hidden
-            to_mid_from_outer(c).wait_recv()
-            inward[c] = (hidden + from_outer[c].astype(jnp.float32)).astype(jnp.bfloat16)
-            to_mid_from_mid(c).start()
-
-        def forward_out(c):
-            to_mid_from_mid(c).wait_recv()
-            hidden = part[c] + from_inner[c].astype(jnp.float32)
-            outward[c] = hidden.astype(jnp.bfloat16)
-            to_outer(c).start()
-            project(c, hidden + from_outer[c].astype(jnp.float32))
+        def step(c, produces, arrives, returns):
+            if arrives:
+                to_mid_from_outer(c).wait_recv()
+                inward[c] = (part[c] + from_outer[c].astype(jnp.float32)).astype(jnp.bfloat16)
+                to_mid_from_mid(c).start()
+            if returns:
+                e = c - LAG
+                to_mid_from_mid(e).wait_recv()
+                hidden = part[e] + from_inner[e].astype(jnp.float32)
+                outward[e] = hidden.astype(jnp.bfloat16)
+                to_outer(e).start()
+            if produces:
+                part[c + LEAD] = partial_hidden(c + LEAD)
+            if returns:
+                project(e, hidden + from_outer[e].astype(jnp.float32))
+
+        @pl.loop(0, LEAD)
+        def _(c):
+            part[c] = partial_hidden(c)
 
         @pl.loop(0, LAG)
         def _(c):
-            forward_in(c)
-
-        @pl.loop(LAG, chunks)
-        def _(c):
-            forward_in(c)
-            forward_out(c - LAG)
-
-        @pl.loop(chunks - LAG, chunks)
-        def _(c):
-            forward_out(c)
+            step(c, True, True, False)
+
+        @pl.loop(LAG, chunks - LEAD)
+        def _(c):
+            step(c, True, True, True)
+
+        @pl.loop(chunks - LEAD, chunks)
+        def _(c):
+            step(c, False, True, True)
+
+        @pl.loop(chunks, chunks + LAG)
+        def _(c):
+            step(c, False, False, True)
 
         @pl.loop(0, chunks)
         def _(c):

time: 47.7 us -> 45.6 us (0.956)
  Pallas kernels: 45.9 us -> 43.8 us
    pallas_call x1, Pallas kernels: 45.9 us -> 43.8 us  [body(): pl.pallas_call(functools.partial(kernel, ctx_size), out_shape=jax.ShapeDt...]
where the time goes in v3:
time: 45.6 us; the launch traced here: 45.4 us
  Pallas kernels  43.8 us (96%)
  local copies, waits for them, and re-layouts  1.57 us (3%)
    pallas_call x1, Pallas kernels, body(): pl.pallas_call(functools.partial(kernel, ctx_size), out_shape=jax.ShapeDt...  43.8 us
    unnamed x1, local copies, waits for them, and re-layouts  1.57 us

profile of v3, /device:TPU:4, one launch (start us, length us, event | category | flops | bytes accessed | tf_op | source)
XLA Modules:
  0.0 45.4 jit_solution(14607188964532159209)
XLA Ops:
  0.0 43.8 %slab.1 = bf16[128,512]{1,0:T(8,128)(2,1)} custom-call(s32[1,2]{1,0:T(1,128)} %index_ref.1, s32[8,128]{1,0:T(8,128)} %bitcast.3, bf16[2,128,128]{2,1,0:T(8,128)(2,1)} %bitcast.2, bf16[256,640]{1,0:T(8,128)(2,1)} %patches.1, bf16[640,4096]{1,0:T(8,128)(2,1)} %merger.1, bf16[4096,768]{1,0:T(8,128)(2,1)} %proj.1), custom_call_target="tpu_custom_call" | custom-call | flops 4000000000 | bytes 12000000 | tf_op jit(solution)/shard_map/slab/pallas_call | solution.py:364
  43.8 1.6 %copy.8 = bf16[128,512]{1,0:T(8,128)(2,1)} copy(bf16[128,512]{1,0:T(8,128)(2,1)} %slab.1) | data formatting | bytes 262144

commit v4 on v3

--- a/solution.py
+++ b/solution.py
@@ -15,6 +15,8 @@
 HALVES = 2
 LAG = 3
 LEAD = 4
+EARLY = 2
+GROUP = 4
 MESH = pl.DeviceIdType.MESH
 
 
@@ -97,6 +99,10 @@
         depth = pl.ds(pl.multiple_of(c * CHUNK, CHUNK), CHUNK)
         return pltpu.make_async_copy(proj.at[depth, :], proj_v.at[c], proj_sem.at[c])
 
+    @pl.loop(0, EARLY)
+    def _(j):
+        merger_copy(j).start()
+
     barrier = pltpu.get_barrier_semaphore()
 
     @pl.loop(0, video_size)
@@ -124,7 +130,7 @@
     def _():
         edge_copy().start()
 
-    @pl.loop(0, pieces)
+    @pl.loop(EARLY, pieces)
     def _(j):
         merger_copy(j).start()
 
@@ -320,24 +326,39 @@
     total = jnp.sum(weights, axis=0, keepdims=True)
     mixed = mix(kv_own[:, HD:], weights)
 
-    def attend(d, state):
+    def attend(first, count, state):
         top, total, mixed = state
-        for h in range(HALVES):
-            kv_copy(d, h).wait_recv()
-        scores = score(kv_in[d, :, :HD])
+        for d in range(count):
+            for h in range(HALVES):
+                kv_copy(first + d, h).wait_recv()
+        slabs = kv_in[pl.ds(first, count)].reshape(count * rows, 2 * HD)
+        scores = score(slabs[:, :HD])
         new_top = jnp.maximum(top, jnp.max(scores, axis=0, keepdims=True))
         factor = jnp.exp(top - new_top)
         weights = jnp.exp(scores - new_top)
         total = total * factor + jnp.sum(weights, axis=0, keepdims=True)
-        mixed = mixed * factor + mix(kv_in[d, :, HD:], weights)
+        mixed = mixed * factor + mix(slabs[:, HD:], weights)
         return new_top, total, mixed
 
-    top, total, mixed = lax.fori_loop(0, earlier, attend, (top, total, mixed))
-    attended = mixed / total
-    for p in range(QPK):
-        out_ref[:, p * HD : (p + 1) * HD] = jnp.transpose(
-            attended[:, p * rows : (p + 1) * rows]
-        ).astype(jnp.bfloat16)
+    groups = earlier // GROUP
+    state = lax.fori_loop(
+        0, groups, lambda g, state: attend(g * GROUP, GROUP, state), (top, total, mixed)
+    )
+    rest = earlier - groups * GROUP
+
+    def write(state):
+        top, total, mixed = state
+        attended = mixed / total
+        for p in range(QPK):
+            out_ref[:, p * HD : (p + 1) * HD] = jnp.transpose(
+                attended[:, p * rows : (p + 1) * rows]
+            )
+
+    for count in range(GROUP):
+
+        @pl.when(rest == count)
+        def _():
+            write(attend(groups * GROUP, count, state) if count else state)
 
     @pl.loop(0, later)
     def _(d):
@@ -363,7 +384,7 @@
     any_space = pl.BlockSpec(memory_space=pl.ANY)
     return pl.pallas_call(
         functools.partial(kernel, ctx_size),
-        out_shape=jax.ShapeDtypeStruct((rows, QPK * HD), bf16),
+        out_shape=jax.ShapeDtypeStruct((rows, QPK * HD), f32),
         in_specs=[
             pl.BlockSpec(memory_space=pltpu.SMEM),
             pl.BlockSpec(memory_space=pltpu.VMEM),
@@ -417,7 +438,7 @@
         patches,
         merger_weight,
         proj_weight,
-    )
+    ).astype(bf16)
 
 
 def solution(mesh):

time: 45.6 us -> 45.1 us (0.989)
  other arithmetic: 0 us -> 1.62 us
  local copies, waits for them, and re-layouts: 1.57 us -> 0 us
  Pallas kernels: 43.8 us -> 43.3 us
    convert_element_type x0 -> x1, other arithmetic: none -> 1.62 us  [body(): return pl.pallas_call(functools.partial(kernel, ctx_size), out_shape=jax....]
    unnamed x1 -> x0, local copies, waits for them, and re-layouts: 1.57 us -> none
    pallas_call x1, Pallas kernels: 43.8 us -> 43.3 us  [body(): pl.pallas_call(functools.partial(kernel, ctx_size), out_shape=jax.ShapeDt...]
where the time goes in v4:
time: 45.1 us; the launch traced here: 44.9 us
  Pallas kernels  43.3 us (96%)
  other arithmetic  1.62 us (4%)
    pallas_call x1, Pallas kernels, body(): pl.pallas_call(functools.partial(kernel, ctx_size), out_shape=jax.ShapeDt...  43.3 us
    convert_element_type x1, other arithmetic, body(): return pl.pallas_call(functools.partial(kernel, ctx_size), out_shape=jax....  1.62 us

profile of v4, /device:TPU:4, one launch (start us, length us, event | category | flops | bytes accessed | tf_op | source)
XLA Modules:
  0.0 44.9 jit_solution(1113987617337672938)
XLA Ops:
  0.0 43.3 %slab.1 = f32[128,512]{1,0:T(8,128)} custom-call(s32[1,2]{1,0:T(1,128)} %index_ref.1, s32[8,128]{1,0:T(8,128)} %bitcast.3, bf16[2,128,128]{2,1,0:T(8,128)(2,1)} %bitcast.2, bf16[256,640]{1,0:T(8,128)(2,1)} %patches.1, bf16[640,4096]{1,0:T(8,128)(2,1)} %merger.1, bf16[4096,768]{1,0:T(8,128)(2,1)} %proj.1), custom_call_target="tpu_custom_call" | custom-call | flops 4000000000 | bytes 12000000 | tf_op jit(solution)/shard_map/slab/pallas_call | solution.py:385
  43.3 1.6 %convert_element_type.3 = bf16[128,512]{1,0:T(8,128)(2,1)} convert(f32[128,512]{1,0:T(8,128)} %slab.1) | non-fusion elementwise | flops 65536 | bytes 393216 | tf_op jit(solution)/shard_map/convert_element_type | solution.py:441

commit v5 on v4

--- a/solution.py
+++ b/solution.py
@@ -11,11 +11,11 @@
 HD = 128
 QPK = 4
 BLK = 128
-CHUNK = 512
+CHUNK = 256
 HALVES = 2
-LAG = 3
-LEAD = 4
-EARLY = 2
+LAG = 5
+LEAD = 6
+EARLY = 4
 GROUP = 4
 MESH = pl.DeviceIdType.MESH
 

time: 45.1 us -> 45.6 us (1.011)
  no operation moved by 1% of the time
where the time goes in v5:
time: 45.6 us; the launch traced here: 45.4 us
  Pallas kernels  43.7 us (96%)
  other arithmetic  1.62 us (4%)
    pallas_call x1, Pallas kernels, body(): pl.pallas_call(functools.partial(kernel, ctx_size), out_shape=jax.ShapeDt...  43.7 us
    convert_element_type x1, other arithmetic, body(): return pl.pallas_call(functools.partial(kernel, ctx_size), out_shape=jax....  1.62 us

profile of v5, /device:TPU:4, one launch (start us, length us, event | category | flops | bytes accessed | tf_op | source)
XLA Modules:
  0.0 45.4 jit_solution(13656470688578612932)
XLA Ops:
  0.0 43.7 %slab.1 = f32[128,512]{1,0:T(8,128)} custom-call(s32[1,2]{1,0:T(1,128)} %index_ref.1, s32[8,128]{1,0:T(8,128)} %bitcast.3, bf16[2,128,128]{2,1,0:T(8,128)(2,1)} %bitcast.2, bf16[256,640]{1,0:T(8,128)(2,1)} %patches.1, bf16[640,4096]{1,0:T(8,128)(2,1)} %merger.1, bf16[4096,768]{1,0:T(8,128)(2,1)} %proj.1), custom_call_target="tpu_custom_call" | custom-call | flops 4000000000 | bytes 12000000 | tf_op jit(solution)/shard_map/slab/pallas_call | solution.py:385
  43.8 1.6 %convert_element_type.3 = bf16[128,512]{1,0:T(8,128)(2,1)} convert(f32[128,512]{1,0:T(8,128)} %slab.1) | non-fusion elementwise | flops 65536 | bytes 393216 | tf_op jit(solution)/shard_map/convert_element_type | solution.py:441

commit v6 on v5

--- a/solution.py
+++ b/solution.py
@@ -13,7 +13,7 @@
 BLK = 128
 CHUNK = 256
 HALVES = 2
-LAG = 5
+LAG = 2
 LEAD = 6
 EARLY = 4
 GROUP = 4
@@ -352,7 +352,7 @@
         for p in range(QPK):
             out_ref[:, p * HD : (p + 1) * HD] = jnp.transpose(
                 attended[:, p * rows : (p + 1) * rows]
-            )
+            ).astype(jnp.bfloat16)
 
     for count in range(GROUP):
 
@@ -368,6 +368,12 @@
     @pl.when(later > 0)
     def _():
         edge_copy().wait_send()
+
+
+def store(attended, out, sem):
+    copy = pltpu.make_async_copy(attended, out, sem)
+    copy.start()
+    copy.wait()
 
 
 def body(ctx_size, patches, merge_index, merge_vals, merger_weight, proj_weight, frame_ids):
@@ -382,9 +388,9 @@
     bf16, f32 = jnp.bfloat16, jnp.float32
     sem = pltpu.SemaphoreType.DMA
     any_space = pl.BlockSpec(memory_space=pl.ANY)
-    return pl.pallas_call(
+    attended = pl.pallas_call(
         functools.partial(kernel, ctx_size),
-        out_shape=jax.ShapeDtypeStruct((rows, QPK * HD), f32),
+        out_shape=jax.ShapeDtypeStruct((rows, QPK * HD), bf16),
         in_specs=[
             pl.BlockSpec(memory_space=pltpu.SMEM),
             pl.BlockSpec(memory_space=pltpu.VMEM),
@@ -438,7 +444,15 @@
         patches,
         merger_weight,
         proj_weight,
-    ).astype(bf16)
+    )
+    return pl.pallas_call(
+        store,
+        out_shape=jax.ShapeDtypeStruct(attended.shape, bf16),
+        in_specs=[pl.BlockSpec(memory_space=pltpu.VMEM)],
+        out_specs=any_space,
+        scratch_shapes=[sem],
+        name="store",
+    )(attended)
 
 
 def solution(mesh):

time: 45.6 us -> 60.5 us (1.33)
  Pallas kernels: 43.7 us -> 60.3 us
  other arithmetic: 1.62 us -> 0 us
    pallas_call x1, Pallas kernels: 43.7 us -> 58.7 us  [body(): pl.pallas_call(functools.partial(kernel, ctx_size), out_shape=jax.ShapeDt...]
    convert_element_type x1 -> x0, other arithmetic: 1.62 us -> none  [body(): return pl.pallas_call(functools.partial(kernel, ctx_size), out_shape=jax....]
    pallas_call x0 -> x1, Pallas kernels: none -> 1.57 us  [body(): pl.pallas_call(store, out_shape=jax.ShapeDtypeStruct(attended.shape, bf16...]
where the time goes in v6:
time: 60.5 us; the launch traced here: 60.3 us
  Pallas kernels  60.3 us (100%)
    pallas_call x1, Pallas kernels, body(): pl.pallas_call(functools.partial(kernel, ctx_size), out_shape=jax.ShapeDt...  58.7 us
    pallas_call x1, Pallas kernels, body(): pl.pallas_call(store, out_shape=jax.ShapeDtypeStruct(attended.shape, bf16...  1.57 us

profile of v6, /device:TPU:4, one launch (start us, length us, event | category | flops | bytes accessed | tf_op | source)
XLA Modules:
  0.0 60.3 jit_solution(15341438176776382171)
XLA Ops:
  0.0 58.7 %slab.1.attended = bf16[128,512]{1,0:T(8,128)(2,1)} custom-call(s32[1,2]{1,0:T(1,128)} %index_ref.1, s32[8,128]{1,0:T(8,128)} %bitcast.3, bf16[2,128,128]{2,1,0:T(8,128)(2,1)} %bitcast.2, bf16[256,640]{1,0:T(8,128)(2,1)} %patches.1, bf16[640,4096]{1,0:T(8,128)(2,1)} %merger.1, bf16[4096,768]{1,0:T(8,128)(2,1)} %proj.1), custom_call_target="tpu_custom_call" | custom-call | flops 4000000000 | bytes 12000000 | tf_op jit(solution)/shard_map/slab/pallas_call | solution.py:391
  58.7 1.6 %store.1 = bf16[128,512]{1,0:T(8,128)(2,1)} custom-call(bf16[128,512]{1,0:T(8,128)(2,1)} %slab.1.attended), custom_call_target="tpu_custom_call" | custom-call | tf_op jit(solution)/shard_map/store/pallas_call | solution.py:448

commit v7 on v5

--- a/solution.py
+++ b/solution.py
@@ -13,8 +13,8 @@
 BLK = 128
 CHUNK = 256
 HALVES = 2
-LAG = 5
-LEAD = 6
+LAG = 8
+LEAD = 8
 EARLY = 4
 GROUP = 4
 MESH = pl.DeviceIdType.MESH
@@ -352,7 +352,7 @@
         for p in range(QPK):
             out_ref[:, p * HD : (p + 1) * HD] = jnp.transpose(
                 attended[:, p * rows : (p + 1) * rows]
-            )
+            ).astype(jnp.bfloat16)
 
     for count in range(GROUP):
 
@@ -384,7 +384,7 @@
     any_space = pl.BlockSpec(memory_space=pl.ANY)
     return pl.pallas_call(
         functools.partial(kernel, ctx_size),
-        out_shape=jax.ShapeDtypeStruct((rows, QPK * HD), f32),
+        out_shape=jax.ShapeDtypeStruct((rows, QPK * HD), bf16),
         in_specs=[
             pl.BlockSpec(memory_space=pltpu.SMEM),
             pl.BlockSpec(memory_space=pltpu.VMEM),
@@ -438,7 +438,7 @@
         patches,
         merger_weight,
         proj_weight,
-    ).astype(bf16)
+    )
 
 
 def solution(mesh):

time: 45.6 us -> 45.8 us (level)
  other arithmetic: 1.62 us -> 0 us
  local copies, waits for them, and re-layouts: 0 us -> 1.57 us
    convert_element_type x1 -> x0, other arithmetic: 1.62 us -> none  [body(): return pl.pallas_call(functools.partial(kernel, ctx_size), out_shape=jax....]
    unnamed x0 -> x1, local copies, waits for them, and re-layouts: none -> 1.57 us
where the time goes in v7:
time: 45.8 us; the launch traced here: 45.6 us
  Pallas kernels  44 us (96%)
  local copies, waits for them, and re-layouts  1.57 us (3%)
    pallas_call x1, Pallas kernels, body(): pl.pallas_call(functools.partial(kernel, ctx_size), out_shape=jax.ShapeDt...  44 us
    unnamed x1, local copies, waits for them, and re-layouts  1.57 us

profile of v7, /device:TPU:4, one launch (start us, length us, event | category | flops | bytes accessed | tf_op | source)
XLA Modules:
  0.0 45.6 jit_solution(15320246115626537703)
XLA Ops:
  0.0 44.0 %slab.1 = bf16[128,512]{1,0:T(8,128)(2,1)} custom-call(s32[1,2]{1,0:T(1,128)} %index_ref.1, s32[8,128]{1,0:T(8,128)} %bitcast.3, bf16[2,128,128]{2,1,0:T(8,128)(2,1)} %bitcast.2, bf16[256,640]{1,0:T(8,128)(2,1)} %patches.1, bf16[640,4096]{1,0:T(8,128)(2,1)} %merger.1, bf16[4096,768]{1,0:T(8,128)(2,1)} %proj.1), custom_call_target="tpu_custom_call" | custom-call | flops 4000000000 | bytes 12000000 | tf_op jit(solution)/shard_map/slab/pallas_call | solution.py:385
  44.1 1.6 %copy.8 = bf16[128,512]{1,0:T(8,128)(2,1)} copy(bf16[128,512]{1,0:T(8,128)(2,1)} %slab.1) | data formatting | bytes 262144

commit v8 on v4

--- a/solution.py
+++ b/solution.py
@@ -326,12 +326,12 @@
     total = jnp.sum(weights, axis=0, keepdims=True)
     mixed = mix(kv_own[:, HD:], weights)
 
-    def attend(first, count, state):
+    def attend(first, count, h, state):
         top, total, mixed = state
         for d in range(count):
-            for h in range(HALVES):
-                kv_copy(first + d, h).wait_recv()
-        slabs = kv_in[pl.ds(first, count)].reshape(count * rows, 2 * HD)
+            kv_copy(first + d, h).wait_recv()
+        slabs = kv_in[pl.ds(first, count), h * part_rows : (h + 1) * part_rows, :]
+        slabs = slabs.reshape(count * part_rows, 2 * HD)
         scores = score(slabs[:, :HD])
         new_top = jnp.maximum(top, jnp.max(scores, axis=0, keepdims=True))
         factor = jnp.exp(top - new_top)
@@ -341,9 +341,11 @@
         return new_top, total, mixed
 
     groups = earlier // GROUP
-    state = lax.fori_loop(
-        0, groups, lambda g, state: attend(g * GROUP, GROUP, state), (top, total, mixed)
-    )
+    state = (top, total, mixed)
+    for h in range(HALVES):
+        state = lax.fori_loop(
+            0, groups, lambda g, state, h=h: attend(g * GROUP, GROUP, h, state), state
+        )
     rest = earlier - groups * GROUP
 
     def write(state):
@@ -352,13 +354,16 @@
         for p in range(QPK):
             out_ref[:, p * HD : (p + 1) * HD] = jnp.transpose(
                 attended[:, p * rows : (p + 1) * rows]
-            )
+            ).astype(jnp.bfloat16)
 
     for count in range(GROUP):
 
         @pl.when(rest == count)
         def _():
-            write(attend(groups * GROUP, count, state) if count else state)
+            last = state
+            for h in range(HALVES if count else 0):
+                last = attend(groups * GROUP, count, h, last)
+            write(last)
 
     @pl.loop(0, later)
     def _(d):
@@ -384,7 +389,7 @@
     any_space = pl.BlockSpec(memory_space=pl.ANY)
     return pl.pallas_call(
         functools.partial(kernel, ctx_size),
-        out_shape=jax.ShapeDtypeStruct((rows, QPK * HD), f32),
+        out_shape=jax.ShapeDtypeStruct((rows, QPK * HD), bf16),
         in_specs=[
             pl.BlockSpec(memory_space=pltpu.SMEM),
             pl.BlockSpec(memory_space=pltpu.VMEM),
@@ -438,7 +443,7 @@
         patches,
         merger_weight,
         proj_weight,
-    ).astype(bf16)
+    )
 
 
 def solution(mesh):

time: 45.1 us -> 44.8 us (level)
  other arithmetic: 1.62 us -> 0 us
  local copies, waits for them, and re-layouts: 0 us -> 1.57 us
    convert_element_type x1 -> x0, other arithmetic: 1.62 us -> none  [body(): return pl.pallas_call(functools.partial(kernel, ctx_size), out_shape=jax....]
    unnamed x0 -> x1, local copies, waits for them, and re-layouts: none -> 1.57 us
where the time goes in v8:
time: 44.8 us; the launch traced here: 44.6 us
  Pallas kernels  43 us (96%)
  local copies, waits for them, and re-layouts  1.57 us (4%)
    pallas_call x1, Pallas kernels, body(): pl.pallas_call(functools.partial(kernel, ctx_size), out_shape=jax.ShapeDt...  43 us
    unnamed x1, local copies, waits for them, and re-layouts  1.57 us

profile of v8, /device:TPU:4, one launch (start us, length us, event | category | flops | bytes accessed | tf_op | source)
XLA Modules:
  0.0 44.6 jit_solution(11474824378552317027)
XLA Ops:
  0.0 43.0 %slab.1 = bf16[128,512]{1,0:T(8,128)(2,1)} custom-call(s32[1,2]{1,0:T(1,128)} %index_ref.1, s32[8,128]{1,0:T(8,128)} %bitcast.3, bf16[2,128,128]{2,1,0:T(8,128)(2,1)} %bitcast.2, bf16[256,640]{1,0:T(8,128)(2,1)} %patches.1, bf16[640,4096]{1,0:T(8,128)(2,1)} %merger.1, bf16[4096,768]{1,0:T(8,128)(2,1)} %proj.1), custom_call_target="tpu_custom_call" | custom-call | flops 4000000000 | bytes 12000000 | tf_op jit(solution)/shard_map/slab/pallas_call | solution.py:390
  43.0 1.6 %copy.8 = bf16[128,512]{1,0:T(8,128)(2,1)} copy(bf16[128,512]{1,0:T(8,128)(2,1)} %slab.1) | data formatting | bytes 262144

commit v9 on v8

--- a/solution.py
+++ b/solution.py
@@ -186,15 +186,19 @@
             {"ctx": position + 1 + d},
         )
 
-    def finish(h):
+    def row_gain(h):
         mean_square = jnp.sum(squares[h], axis=1, keepdims=True) * (1.0 / hid)
-        gain = lax.rsqrt(mean_square + 1e-06)
-        kv_own[part_span(h), :] = (projected[h, :, QPK * HD :] * gain).astype(jnp.bfloat16)
+        return lax.rsqrt(mean_square + 1e-06)
+
+    def send_kv(h):
+        kv_own[part_span(h), :] = (projected[h, :, QPK * HD :] * row_gain(h)).astype(jnp.bfloat16)
 
         @pl.loop(0, later)
-        def _(d):
-            kv_copy(d, h).start()
-
+        def _(i):
+            kv_copy(later - 1 - i, h).start()
+
+    def keep_queries(h):
+        gain = row_gain(h)
         for p in range(QPK):
             at = pl.ds(pl.multiple_of(p * rows + h * part_rows, part_rows), part_rows)
             queries[at, :] = (projected[h, :, p * HD : (p + 1) * HD] * gain).astype(jnp.bfloat16)
@@ -213,11 +217,21 @@
         def _():
             proj_copy(j).wait()
 
-        projected[h] += jnp.dot(hidden, proj_v[j], preferred_element_type=jnp.float32)
+        projected[h, :, QPK * HD :] += jnp.dot(
+            hidden, proj_v[j, :, QPK * HD :], preferred_element_type=jnp.float32
+        )
 
         @pl.when(j == pieces - 1)
         def _():
-            finish(h)
+            send_kv(h)
+
+        projected[h, :, : QPK * HD] += jnp.dot(
+            hidden, proj_v[j, :, : QPK * HD], preferred_element_type=jnp.float32
+        )
+
+        @pl.when(j == pieces - 1)
+        def _():
+            keep_queries(h)
 
     def to_mid_from_outer(c):
         return remote(

time: 44.8 us -> 44.7 us (level)
  no operation moved by 1% of the time
where the time goes in v9:
time: 44.7 us; the launch traced here: 44.5 us
  Pallas kernels  42.9 us (96%)
  local copies, waits for them, and re-layouts  1.57 us (4%)
    pallas_call x1, Pallas kernels, body(): pl.pallas_call(functools.partial(kernel, ctx_size), out_shape=jax.ShapeDt...  42.9 us
    unnamed x1, local copies, waits for them, and re-layouts  1.57 us

profile of v9, /device:TPU:4, one launch (start us, length us, event | category | flops | bytes accessed | tf_op | source)
XLA Modules:
  0.0 44.5 jit_solution(12052584603341080482)
XLA Ops:
  0.0 42.9 %slab.1 = bf16[128,512]{1,0:T(8,128)(2,1)} custom-call(s32[1,2]{1,0:T(1,128)} %index_ref.1, s32[8,128]{1,0:T(8,128)} %bitcast.3, bf16[2,128,128]{2,1,0:T(8,128)(2,1)} %bitcast.2, bf16[256,640]{1,0:T(8,128)(2,1)} %patches.1, bf16[640,4096]{1,0:T(8,128)(2,1)} %merger.1, bf16[4096,768]{1,0:T(8,128)(2,1)} %proj.1), custom_call_target="tpu_custom_call" | custom-call | flops 4000000000 | bytes 12000000 | tf_op jit(solution)/shard_map/slab/pallas_call | solution.py:404
  42.9 1.6 %copy.8 = bf16[128,512]{1,0:T(8,128)(2,1)} copy(bf16[128,512]{1,0:T(8,128)(2,1)} %slab.1) | data formatting | bytes 262144

commit v10 on v9

--- a/solution.py
+++ b/solution.py
@@ -11,11 +11,11 @@
 HD = 128
 QPK = 4
 BLK = 128
-CHUNK = 512
+CHUNK = 256
 HALVES = 2
-LAG = 3
-LEAD = 4
-EARLY = 2
+LAG = 6
+LEAD = 6
+EARLY = 4
 GROUP = 4
 MESH = pl.DeviceIdType.MESH
 

time: 44.7 us -> 45.1 us (level)
  Pallas kernels: 42.9 us -> 43.4 us
where the time goes in v10:
time: 45.1 us; the launch traced here: 45 us
  Pallas kernels  43.4 us (96%)
  local copies, waits for them, and re-layouts  1.57 us (3%)
    pallas_call x1, Pallas kernels, body(): pl.pallas_call(functools.partial(kernel, ctx_size), out_shape=jax.ShapeDt...  43.4 us
    unnamed x1, local copies, waits for them, and re-layouts  1.57 us

profile of v10, /device:TPU:4, one launch (start us, length us, event | category | flops | bytes accessed | tf_op | source)
XLA Modules:
  0.0 45.0 jit_solution(17334440375041948911)
XLA Ops:
  0.0 43.4 %slab.1 = bf16[128,512]{1,0:T(8,128)(2,1)} custom-call(s32[1,2]{1,0:T(1,128)} %index_ref.1, s32[8,128]{1,0:T(8,128)} %bitcast.3, bf16[2,128,128]{2,1,0:T(8,128)(2,1)} %bitcast.2, bf16[256,640]{1,0:T(8,128)(2,1)} %patches.1, bf16[640,4096]{1,0:T(8,128)(2,1)} %merger.1, bf16[4096,768]{1,0:T(8,128)(2,1)} %proj.1), custom_call_target="tpu_custom_call" | custom-call | flops 4000000000 | bytes 12000000 | tf_op jit(solution)/shard_map/slab/pallas_call | solution.py:404
  43.4 1.6 %copy.8 = bf16[128,512]{1,0:T(8,128)(2,1)} copy(bf16[128,512]{1,0:T(8,128)(2,1)} %slab.1) | data formatting | bytes 262144
